TPU v7x, 32 devices: a whole 2x2x4 slice. The times are simulated.
32 devices in a mesh: dp: 4 (over y, x), tensor: 4 (over z), section: 2 (over core).
Axes of the slice: x: 2, y: 2, z: 4, core: 2. Of those that a mesh axis runs over, the one named last changes fastest.
Arguments:
- train_act: bfloat16 [2, 1024, 8192], P('section', ('dp', 'tensor')), may hold values from -6 to 6
- train_grad: bfloat16 [2, 1024, 28672], P('section', 'dp', 'tensor'), may hold values from -6 to 6
- val_act: bfloat16 [2, 16, 8192], P('section', 'dp'), may hold values from -6 to 6
- val_grad: bfloat16 [2, 16, 28672], P('section', 'dp', 'tensor'), may hold values from -6 to 6
Outputs:
- scores: float32 [1024], P(('dp', 'tensor', 'section'))
All inputs are finite; a program needn't handle non-finite values.
Results may differ from a plain program's by a relative error of at most 0.0003.
Values may be sent and summed in bfloat16 or wider, within the bound.
A program may use at most 64 MiB of HBM per device.

v0:
```python
import math

import jax
import jax.numpy as jnp
from jax import lax
from jax.sharding import PartitionSpec as P


def gram_of(left, right):
    return lax.dot_general(
        left, right, (((1,), (1,)), ((), ())), preferred_element_type=jnp.float32
    )


def local(train_act, train_grad, val_act, val_grad):
    own_rows = train_act[0]
    grad_rows = train_grad[0]
    width = own_rows.shape[1]
    groups = lax.axis_size("tensor")
    hidden = grad_rows.shape[1] * groups
    val_total = val_act.shape[1] * lax.axis_size("dp")
    factor = 1.0 / math.sqrt(width * hidden * val_total)
    val_left = val_act[0]
    act_buf = gram_of(own_rows, lax.all_gather(val_left, "dp", axis=0, tiled=True))
    grad_buf = gram_of(grad_rows, lax.all_gather(val_grad[0], "dp", axis=0, tiled=True))
    grad_gram = lax.psum_scatter(grad_buf, "tensor", scatter_dimension=0, tiled=True)
    partial_scores = jnp.sum(act_buf * grad_gram, axis=1)
    return lax.psum_scatter(partial_scores * factor, "section", scatter_dimension=0, tiled=True)


def solution(mesh):
    in_specs = (
        P("section", ("dp", "tensor"), None),
        P("section", "dp", "tensor"),
        P("section", "dp", None),
        P("section", "dp", "tensor"),
    )
    out_specs = P(("dp", "tensor", "section"))
    return jax.shard_map(local, mesh=mesh, in_specs=in_specs, out_specs=out_specs, check_vma=False)
```

profile of v0, /device:TPU:0, one launch (start us, length us, event | category | flops | bytes accessed | tf_op | source)
XLA Modules:
  0.0 53.5 jit_solution(17673896674243603457)
XLA Ops:
  6.5 0.0 copy-start
  6.5 0.0 copy-start.2
  6.5 0.0 copy-start.1
  6.5 0.0 reduce-scatter.4.cloned.1.call-start
  6.5 1.0 %copy.8 = bf16[1,4,7168]{2,0,1:T(2,128)(2,1)S(1)} copy(bf16[1,4,7168]{2,1,0:T(4,128)(2,1)} %param.7) | data formatting | bytes 114688 | tf_op args[3]
  7.6 11.2 %all-gather.1 = bf16[1,16,7168]{2,0,1:T(2,128)(2,1)S(1)} all-gather(bf16[1,4,7168]{2,0,1:T(2,128)(2,1)S(1)} %copy.8), channel_id=3, replica_groups=mesh['dp'=4,'tensor'=4,'section'=2] {'dp'}, dimensions={1}, use_global_device_ids=true | all-gather | bytes 286720 | tf_op jit(solution)/shard_map/all_gather | solution.py:25
  18.8 3.8 %fusion = f32[256,16]{1,0:T(8,128)} fusion(bf16[1,256,7168]{2,1,0:T(8,128)(2,1)} %param.5, bf16[1,16,7168]{2,0,1:T(2,128)(2,1)S(1)} %all-gather.1), kind=kOutput, calls=%fused_computation | convolution fusion | flops 58720256 | bytes 3915776
  22.6 0.0 reduce-scatter.4.cloned.1.call-update
  22.6 0.0 copy-done.1
  22.6 0.1 copy.7
  22.7 0.0 copy-done.2
  22.7 0.6 %dynamic-slice = u32[1]{0:T(128)} dynamic-slice(u32[32]{0:T(128)S(1)} %copy-done.2, u32[]{:T(128)S(6)} %add.5), dynamic_slice_sizes={1} | dynamic-slice | bytes 12
  24.0 10.2 %all-gather = bf16[1,16,8192]{2,0,1:T(2,128)(2,1)S(1)} all-gather(bf16[1,4,8192]{2,0,1:T(2,128)(2,1)S(1)} %copy.7), channel_id=2, replica_groups=mesh['dp'=4,'tensor'=4,'section'=2] {'dp'}, dimensions={1}, use_global_device_ids=true | all-gather | bytes 327680 | tf_op jit(solution)/shard_map/all_gather | solution.py:24
  34.2 8.1 %reduce-scatter.4.cloned.1.call-done = f32[64,16]{1,0:T(8,128)} async-done(((f32[256,16]{1,0:T(8,128)}), f32[64,16]{1,0:T(8,128)}) %reduce-scatter.4.cloned.1.call-update) | async-done | bytes 4112
  42.2 0.8 %copy.10 = f32[64,16]{0,1:T(8,128)S(1)} copy(f32[64,16]{1,0:T(8,128)} %reduce-scatter.4.cloned.1.call-done) | data formatting | bytes 8192
  43.0 0.0 copy-done
  43.0 0.5 %fusion.2 = f32[64]{0:T(128)S(1)} fusion(f32[64,16]{0,1:T(8,128)S(1)} %copy.10, bf16[1,64,8192]{2,1,0:T(8,128)(2,1)S(1)} %copy-done, bf16[1,16,8192]{2,0,1:T(2,128)(2,1)S(1)} %all-gather), kind=kOutput, calls=%fused_computation.3 | convolution fusion | flops 16779200 | bytes 1315072 | tf_op jit(solution)/shard_map/dot_general | solution.py:10
  43.6 2.5 %all-reduce = f32[64]{0:T(128)S(1)} all-reduce(f32[64]{0:T(128)S(1)} %broadcast_multiply_fusion), channel_id=5, replica_groups=mesh['dp'=4,'tensor'=4,'section'=2] {'section'}, use_global_device_ids=true, to_apply=%region_2.0.clone | all-reduce | flops 64 | bytes 512
  46.1 0.6 %dynamic-slice.1 = f32[32]{0:T(128)} dynamic-slice(f32[64]{0:T(128)S(1)} %all-reduce, u32[]{:T(128)S(6)} %multiply.1), dynamic_slice_sizes={32} | dynamic-slice | bytes 260
  (1 shorter events, 0.0 us)
Async XLA Ops:
  6.5 36.5 %copy-start = (bf16[1,64,8192]{2,1,0:T(8,128)(2,1)S(1)}, bf16[1,64,8192]{2,1,0:T(8,128)(2,1)}, u32[]{:S(2)}) copy-start(bf16[1,64,8192]{2,1,0:T(8,128)(2,1)} %param.4) | copy-start | bytes 3145732
  6.5 16.2 %copy-start.2 = (u32[32]{0:T(128)S(1)}, u32[32]{0:T(128)}, u32[]{:S(2)}) copy-start(u32[32]{0:T(128)} %constant.10) | copy-start | bytes 388
  6.5 16.1 %copy-start.1 = (bf16[1,4,8192]{2,1,0:T(4,128)(2,1)S(1)}, bf16[1,4,8192]{2,1,0:T(4,128)(2,1)}, u32[]{:S(2)}) copy-start(bf16[1,4,8192]{2,1,0:T(4,128)(2,1)} %param.6) | copy-start | bytes 196612
  6.5 35.7 %reduce-scatter.4.cloned.1.call-start = ((), (), s32[]{:S(2)}) async-start(), calls=%async_computation.1 | async-start | bytes 163840
Sparse Core Ops, SparseCore 0:
  22.7 19.4 reduce-scatter.3
where the time goes:
time: 53.8 us; the launch traced here: 53.5 us
  blocking collectives  23.9 us (44%)
  between operations  14.1 us (26%)
  waiting for transfers between devices  8.07 us (15%)
  matrix products  4.31 us (8%)
  local copies, waits for them, and re-layouts  3.13 us (6%)
    all_gather x1, blocking collectives, local(): lax.all_gather(val_grad[0], 'dp', axis=0, tiled=True)  11.2 us
    all_gather x1, blocking collectives, local(): lax.all_gather(val_left, 'dp', axis=0, tiled=True)  10.2 us
    unnamed x2, waiting for transfers between devices  8.07 us
    unnamed x1, matrix products  3.76 us
    unnamed x11, local copies, waits for them, and re-layouts  3.13 us
    unnamed x1, blocking collectives  2.47 us
  transfers between devices with their start and end apart: 1, of which 1 were waited for; matrix products, arithmetic and copies ran while one was open for 1% of the time, Pallas kernels for 0%

commit v1 on v0

v1 whole, which is shorter than its diff:
```python
import functools
import math

import jax
import jax.numpy as jnp
from jax import lax
from jax.experimental import pallas as pl
from jax.experimental.pallas import tpu as pltpu
from jax.sharding import PartitionSpec as P

LANES = 128
MIB = 1 << 20


def pieces(width, wanted):
    return max(c for c in range(1, wanted + 1) if width % (c * LANES) == 0)


def gram_of(left, right):
    return lax.dot_general(
        left, right, (((1,), (1,)), ((), ())), preferred_element_type=jnp.float32
    )


def kernel(
    sizes, factor, ta_hbm, tg_hbm, va_hbm, vg_hbm, out_ref,
    ta, tg, va, vg, ag_own, ag, ps_own, ps,
    ta_sem, tg_sem, va_sem, vg_sem, va_send, va_recv, vg_send, vg_recv,
    ag_send, ag_recv, ps_send, ps_recv,
):
    dp, tensor, section, ca, cg = sizes
    d, z, c = (lax.axis_index(a) for a in ("dp", "tensor", "section"))
    own = ta_hbm.shape[1]
    wa, wg = va.shape[2] // ca, vg.shape[2] // cg
    ranks = tensor * section

    load_va = pltpu.make_async_copy(va_hbm.at[0], va.at[d], va_sem)
    load_vg = pltpu.make_async_copy(vg_hbm.at[0], vg.at[d], vg_sem)
    load_ta = pltpu.make_async_copy(ta_hbm.at[0], ta, ta_sem)
    load_tg = pltpu.make_async_copy(tg_hbm.at[0], tg, tg_sem)
    for load in (load_va, load_vg, load_ta, load_tg):
        load.start()

    def group(r):
        dz, dc = r // section, r % section
        return {"tensor": lax.rem(z + dz, tensor), "section": lax.rem(c + dc, section)}

    barrier = pltpu.get_barrier_semaphore()
    for r in range(1, dp):
        pl.semaphore_signal(barrier, inc=1, device_id={"dp": lax.rem(d + r, dp)})
    for r in range(1, ranks):
        pl.semaphore_signal(barrier, inc=1, device_id=group(r))
    pl.semaphore_wait(barrier, dp - 1 + ranks - 1)

    def val_copy(buf, send, recv, r, k, width, slot):
        piece = buf.at[slot, :, pl.ds(k * width, width)]
        return pltpu.make_async_remote_copy(
            src_ref=piece, dst_ref=piece,
            send_sem=send.at[r - 1, k], recv_sem=recv.at[r - 1, k],
            device_id={"dp": lax.rem(d + r, dp)},
        )

    load_va.wait()
    for k in range(ca):
        for r in range(1, dp):
            val_copy(va, va_send, va_recv, r, k, wa, d).start()
    load_vg.wait()
    for k in range(cg):
        for r in range(1, dp):
            val_copy(vg, vg_send, vg_recv, r, k, wg, d).start()

    def gram(buf, send, recv, train, count, width):
        total = None
        for k in range(count):
            for r in range(1, dp):
                val_copy(buf, send, recv, r, k, width, lax.rem(d + dp - r, dp)).wait_recv()
            cols = pl.ds(k * width, width)
            left = jnp.concatenate([buf[j, :, cols] for j in range(dp)], axis=0)
            term = gram_of(left, train[:, cols])
            total = term if total is None else total + term
        return total

    load_ta.wait()
    act = gram(va, va_send, va_recv, ta, ca, wa)
    ag_own[...] = jnp.zeros_like(ag_own)
    ag_own[:, 0:own] = act

    def act_copy(r, slot):
        return pltpu.make_async_remote_copy(
            src_ref=ag_own, dst_ref=ag.at[slot],
            send_sem=ag_send.at[r - 1], recv_sem=ag_recv.at[r - 1],
            device_id={"tensor": lax.rem(z + r, tensor)},
        )

    for r in range(1, tensor):
        act_copy(r, z).start()
    ag[z] = ag_own[...]

    load_tg.wait()
    grad = gram(vg, vg_send, vg_recv, tg, cg, wg)

    for r in range(1, tensor):
        act_copy(r, lax.rem(z + tensor - r, tensor)).wait_recv()
    act_all = jnp.concatenate([ag[j, :, 0:own] for j in range(tensor)], axis=1)
    ps_own[...] = jnp.sum(act_all * grad, axis=0, keepdims=True) * factor

    def score_copy(r, slot):
        return pltpu.make_async_remote_copy(
            src_ref=ps_own, dst_ref=ps.at[slot],
            send_sem=ps_send.at[r - 1], recv_sem=ps_recv.at[r - 1],
            device_id=group(r),
        )

    for r in range(1, ranks):
        score_copy(r, r - 1).start()
    total = ps_own[...]
    for r in range(1, ranks):
        score_copy(r, r - 1).wait_recv()
        total = total + ps[r - 1]
    share = total.shape[1] // ranks
    mine = z * section + c
    result = total[:, 0:share]
    for b in range(1, ranks):
        result = jnp.where(mine == b, total[:, b * share : (b + 1) * share], result)
    out_ref[...] = result

    for r in range(1, dp):
        for k in range(ca):
            val_copy(va, va_send, va_recv, r, k, wa, d).wait_send()
        for k in range(cg):
            val_copy(vg, vg_send, vg_recv, r, k, wg, d).wait_send()
    for r in range(1, tensor):
        act_copy(r, z).wait_send()
    for r in range(1, ranks):
        score_copy(r, r - 1).wait_send()


def solution(mesh):
    dp, tensor, section = (mesh.shape[a] for a in ("dp", "tensor", "section"))

    def local(train_act, train_grad, val_act, val_grad):
        own, width = train_act.shape[1:]
        tokens, hidden = train_grad.shape[1:]
        val = val_act.shape[1]
        factor = 1.0 / math.sqrt(width * hidden * tensor * val * dp)
        ca, cg = pieces(width, 2), pieces(hidden, 4)
        ranks = tensor * section
        share = tokens // ranks
        own_lanes = -(-own // LANES) * LANES
        dma = pltpu.SemaphoreType.DMA
        bf16, f32 = jnp.bfloat16, jnp.float32
        scores = pl.pallas_call(
            functools.partial(kernel, (dp, tensor, section, ca, cg), factor),
            out_shape=jax.ShapeDtypeStruct((1, share), f32),
            in_specs=[pl.BlockSpec(memory_space=pl.ANY)] * 4,
            out_specs=pl.BlockSpec(memory_space=pltpu.VMEM),
            scratch_shapes=[
                pltpu.VMEM((own, width), bf16),
                pltpu.VMEM((tokens, hidden), bf16),
                pltpu.VMEM((dp, val, width), bf16),
                pltpu.VMEM((dp, val, hidden), bf16),
                pltpu.VMEM((val * dp, own_lanes), f32),
                pltpu.VMEM((tensor, val * dp, own_lanes), f32),
                pltpu.VMEM((1, tokens), f32),
                pltpu.VMEM((ranks - 1, 1, tokens), f32),
                dma, dma, dma, dma,
                dma((dp - 1, ca)), dma((dp - 1, ca)),
                dma((dp - 1, cg)), dma((dp - 1, cg)),
                dma((tensor - 1,)), dma((tensor - 1,)),
                dma((ranks - 1,)), dma((ranks - 1,)),
            ],
            compiler_params=pltpu.CompilerParams(
                collective_id=0, has_side_effects=True, vmem_limit_bytes=56 * MIB
            ),
        )(train_act, train_grad, val_act, val_grad)
        return scores.reshape(share)

    in_specs = (
        P("section", ("dp", "tensor"), None),
        P("section", "dp", "tensor"),
        P("section", "dp", None),
        P("section", "dp", "tensor"),
    )
    out_specs = P(("dp", "tensor", "section"))
    return jax.shard_map(local, mesh=mesh, in_specs=in_specs, out_specs=out_specs, check_vma=False)
```

time: 53.8 us -> 21.8 us (0.41)
  blocking collectives: 23.9 us -> 0 us
  Pallas kernels: 0 us -> 20.5 us
  between operations: 14.1 us -> 0.01 us
  waiting for transfers between devices: 8.07 us -> 0 us
  matrix products: 4.31 us -> 0 us
  local copies, waits for them, and re-layouts: 3.13 us -> 1.19 us
    all_gather x2 -> x0, blocking collectives: 21.4 us -> none  [the longest x1 11.2 us: local(): lax.all_gather(val_grad[0], 'dp', axis=0, tiled=True)]
    pallas_call x0 -> x1, Pallas kernels: none -> 20.5 us  [local(): pl.pallas_call(functools.partial(kernel, (dp, tensor, section, ca, cg), f...]
    unnamed x2 -> x0, waiting for transfers between devices: 8.07 us -> none
    unnamed x1 -> x0, matrix products: 3.76 us -> none
    unnamed x1 -> x0, blocking collectives: 2.47 us -> none
    unnamed x11 -> x1, local copies, waits for them, and re-layouts: 3.13 us -> 1.19 us
    dot_general x1 -> x0, matrix products: 0.55 us -> none  [gram_of(): lax.dot_general(left, right, (((1,), (1,)), ((), ())), preferred_element_...]
  transfers between devices with their start and end apart: 1 -> 0, of which waited for: 1 -> 0; matrix products, arithmetic and copies ran while one was open for 1% -> 0% of each run, Pallas kernels for 0% -> 0%
where the time goes in v1:
time: 21.8 us; the launch traced here: 21.7 us
  Pallas kernels  20.5 us (94%)
  local copies, waits for them, and re-layouts  1.19 us (5%)
    pallas_call x1, Pallas kernels, local(): pl.pallas_call(functools.partial(kernel, (dp, tensor, section, ca, cg), f...  20.5 us
    unnamed x1, local copies, waits for them, and re-layouts  1.19 us

profile of v1, /device:TPU:0, one launch (start us, length us, event | category | flops | bytes accessed | tf_op | source)
XLA Modules:
  0.0 21.7 jit_solution(7220561078279319340)
XLA Ops:
  0.0 20.5 %shard_map.46 = f32[1,32]{1,0:T(1,128)} custom-call(bf16[1,64,8192]{2,1,0:T(8,128)(2,1)} %ta_hbm.1, bf16[1,256,7168]{2,1,0:T(8,128)(2,1)} %tg_hbm.1, bf16[1,4,8192]{2,1,0:T(4,128)(2,1)} %va_hbm.1, bf16[1,4,7168]{2,1,0:T(4,128)(2,1)} %vg_hbm.1), custom_call_target="tpu_custom_call" | custom-call | tf_op jit(solution)/shard_map/pallas_call | solution.py:152
  20.5 1.2 %copy.6 = f32[32]{0:T(128)} copy(f32[32]{0:T(128)} %bitcast.1) | data formatting | bytes 256

commit v2 on v1

v2 whole, which is shorter than its diff:
```python
import functools
import math

import jax
import jax.numpy as jnp
from jax import lax
from jax.experimental import pallas as pl
from jax.experimental.pallas import tpu as pltpu
from jax.sharding import PartitionSpec as P

LANES = 128
MIB = 1 << 20


def pieces(width, wanted):
    return max(c for c in range(1, wanted + 1) if width % (c * LANES) == 0)


def gram_of(left, right):
    return lax.dot_general(
        left, right, (((1,), (1,)), ((), ())), preferred_element_type=jnp.float32
    )


def peer(me, r):
    bit = 1
    while bit <= r:
        if r & bit:
            me = me + bit * (1 - 2 * ((me // bit) % 2))
        bit *= 2
    return me


def kernel(
    sizes, factor, ta_hbm, tg_hbm, va_hbm, vg_hbm, out_ref,
    ta, tg, va, vg, gz_own, gz, ps_own, ps,
    ta_sem, tg_sem, va_sem, vg_sem, va_send, va_recv, vg_send, vg_recv,
    gz_send, gz_recv, ps_send, ps_recv, dp_relay, z_relay,
):
    dp, tensor, section, ca, cg = sizes
    d, z, c = (lax.axis_index(a) for a in ("dp", "tensor", "section"))
    own = ta_hbm.shape[1]
    wa, wg = va.shape[2] // ca, vg.shape[2] // cg
    square = dp == 4
    near = (1, 2) if square else tuple(range(1, dp))
    far = (3,) if square else ()

    def dp_peer(r):
        if square:
            return peer(d, r), peer(d, r)
        return lax.rem(d + r, dp), lax.rem(d + dp - r, dp)

    def chain(signal):
        for step, there in ((-1, z > 0), (1, z < tensor - 1)):
            pl.when(there)(functools.partial(signal, {"tensor": z + step}))
        return jnp.where(z > 0, 1, 0) + jnp.where(z < tensor - 1, 1, 0)

    load_va = pltpu.make_async_copy(va_hbm.at[0], va.at[d], va_sem)
    load_vg = pltpu.make_async_copy(vg_hbm.at[0], vg.at[d], vg_sem)
    load_ta = pltpu.make_async_copy(ta_hbm.at[0], ta, ta_sem)
    load_tg = pltpu.make_async_copy(tg_hbm.at[0], tg, tg_sem)
    for load in (load_vg, load_va, load_tg, load_ta):
        load.start()

    barrier = pltpu.get_barrier_semaphore()
    greeted = chain(lambda there: pl.semaphore_signal(barrier, inc=1, device_id=there))
    for r in near:
        pl.semaphore_signal(barrier, inc=1, device_id={"dp": dp_peer(r)[0]})
    for r in range(1, section):
        pl.semaphore_signal(barrier, inc=1, device_id={"section": lax.rem(c + r, section)})
    pl.semaphore_wait(barrier, greeted + len(near) + section - 1)

    def val_copy(buf, send, recv, r, k, width, incoming=False):
        piece = buf.at[dp_peer(r)[1] if incoming else d, :, pl.ds(k * width, width)]
        return pltpu.make_async_remote_copy(
            src_ref=piece, dst_ref=piece,
            send_sem=send.at[r - 1, k], recv_sem=recv.at[r - 1, k],
            device_id={"dp": dp_peer(r)[0]},
        )

    if square:
        pl.semaphore_signal(dp_relay, inc=1, device_id={"dp": peer(d, 1)})
    if tensor > 2:
        chain(lambda there: pl.semaphore_signal(z_relay.at[0], inc=1, device_id=there))
    load_vg.wait()
    for k in range(cg):
        for r in near:
            val_copy(vg, vg_send, vg_recv, r, k, wg).start()
    if square:
        pl.semaphore_wait(dp_relay, 1)
    for k in range(cg):
        for r in far:
            val_copy(vg, vg_send, vg_recv, r, k, wg).start()
    load_va.wait()
    for k in range(ca):
        for r in near + far:
            val_copy(va, va_send, va_recv, r, k, wa).start()
    for s in range(tensor - 2):
        pl.semaphore_wait(z_relay.at[s], greeted)
        if s < tensor - 3:
            chain(lambda there, s=s: pl.semaphore_signal(z_relay.at[s + 1], inc=1, device_id=there))
    gz_own[...] = jnp.zeros_like(gz_own)
    ps_own[...] = jnp.zeros_like(ps_own)

    def gram(buf, send, recv, train, count, width):
        total = None
        for k in range(count):
            for r in near + far:
                val_copy(buf, send, recv, r, k, width, incoming=True).wait_recv()
            cols = pl.ds(k * width, width)
            left = jnp.concatenate([buf[j, :, cols] for j in range(dp)], axis=0)
            term = gram_of(left, train[:, cols])
            total = term if total is None else total + term
        return total

    load_tg.wait()
    grad = gram(vg, vg_send, vg_recv, tg, cg, wg)
    for j in range(tensor):
        gz_own[j, :, 0:own] = grad[:, j * own : (j + 1) * own]

    def grad_copy(r):
        there = lax.rem(z + r, tensor)
        return pltpu.make_async_remote_copy(
            src_ref=gz_own.at[there], dst_ref=gz.at[r - 1],
            send_sem=gz_send.at[r - 1], recv_sem=gz_recv.at[r - 1],
            device_id={"tensor": there},
        )

    for r in range(1, tensor):
        grad_copy(r).start()

    load_ta.wait()
    act = gram(va, va_send, va_recv, ta, ca, wa)

    grad_sum = gz_own[z]
    for r in range(1, tensor):
        grad_copy(r).wait_recv()
        grad_sum = grad_sum + gz[r - 1]
    scores = jnp.sum(act * grad_sum[:, 0:own], axis=0, keepdims=True) * factor
    ps_own[:, 0:own] = scores

    def score_copy(r):
        return pltpu.make_async_remote_copy(
            src_ref=ps_own, dst_ref=ps.at[r - 1],
            send_sem=ps_send.at[r - 1], recv_sem=ps_recv.at[r - 1],
            device_id={"section": lax.rem(c + r, section)},
        )

    for r in range(1, section):
        score_copy(r).start()
    for r in range(1, section):
        score_copy(r).wait_recv()
        scores = scores + ps[r - 1][:, 0:own]
    share = own // section
    result = scores[:, 0:share]
    for b in range(1, section):
        result = jnp.where(c == b, scores[:, b * share : (b + 1) * share], result)
    out_ref[...] = result

    for r in near + far:
        for k in range(cg):
            val_copy(vg, vg_send, vg_recv, r, k, wg).wait_send()
        for k in range(ca):
            val_copy(va, va_send, va_recv, r, k, wa).wait_send()
    for r in range(1, tensor):
        grad_copy(r).wait_send()
    for r in range(1, section):
        score_copy(r).wait_send()


def solution(mesh):
    dp, tensor, section = (mesh.shape[a] for a in ("dp", "tensor", "section"))

    def local(train_act, train_grad, val_act, val_grad):
        own, width = train_act.shape[1:]
        tokens, hidden = train_grad.shape[1:]
        val = val_act.shape[1]
        factor = 1.0 / math.sqrt(width * hidden * tensor * val * dp)
        ca, cg = pieces(width, 1), pieces(hidden, 2)
        share = tokens // (tensor * section)
        own_lanes = -(-own // LANES) * LANES
        dma = pltpu.SemaphoreType.DMA
        bf16, f32 = jnp.bfloat16, jnp.float32
        scores = pl.pallas_call(
            functools.partial(kernel, (dp, tensor, section, ca, cg), factor),
            out_shape=jax.ShapeDtypeStruct((1, share), f32),
            in_specs=[pl.BlockSpec(memory_space=pl.ANY)] * 4,
            out_specs=pl.BlockSpec(memory_space=pltpu.VMEM),
            scratch_shapes=[
                pltpu.VMEM((own, width), bf16),
                pltpu.VMEM((tokens, hidden), bf16),
                pltpu.VMEM((dp, val, width), bf16),
                pltpu.VMEM((dp, val, hidden), bf16),
                pltpu.VMEM((tensor, val * dp, own_lanes), f32),
                pltpu.VMEM((tensor - 1, val * dp, own_lanes), f32),
                pltpu.VMEM((1, own_lanes), f32),
                pltpu.VMEM((section - 1, 1, own_lanes), f32),
                dma, dma, dma, dma,
                dma((dp - 1, ca)), dma((dp - 1, ca)),
                dma((dp - 1, cg)), dma((dp - 1, cg)),
                dma((tensor - 1,)), dma((tensor - 1,)),
                dma((section - 1,)), dma((section - 1,)),
                pltpu.SemaphoreType.REGULAR,
                pltpu.SemaphoreType.REGULAR((max(tensor - 2, 1),)),
            ],
            compiler_params=pltpu.CompilerParams(
                collective_id=0, has_side_effects=True, vmem_limit_bytes=56 * MIB
            ),
        )(train_act, train_grad, val_act, val_grad)
        return scores.reshape(share)

    in_specs = (
        P("section", ("dp", "tensor"), None),
        P("section", "dp", "tensor"),
        P("section", "dp", None),
        P("section", "dp", "tensor"),
    )
    out_specs = P(("dp", "tensor", "section"))
    return jax.shard_map(local, mesh=mesh, in_specs=in_specs, out_specs=out_specs, check_vma=False)
```

time: 21.8 us -> 19.8 us (0.908)
  Pallas kernels: 20.5 us -> 18.4 us
    pallas_call x1, Pallas kernels: 20.5 us -> 18.4 us  [local(): pl.pallas_call(functools.partial(kernel, (dp, tensor, section, ca, cg), f...]
where the time goes in v2:
time: 19.8 us; the launch traced here: 19.6 us
  Pallas kernels  18.4 us (93%)
  local copies, waits for them, and re-layouts  1.19 us (6%)
    pallas_call x1, Pallas kernels, local(): pl.pallas_call(functools.partial(kernel, (dp, tensor, section, ca, cg), f...  18.4 us
    unnamed x1, local copies, waits for them, and re-layouts  1.19 us

profile of v2, /device:TPU:0, one launch (start us, length us, event | category | flops | bytes accessed | tf_op | source)
XLA Modules:
  0.0 19.6 jit_solution(14904609441721018524)
XLA Ops:
  0.0 18.4 %shard_map.46 = f32[1,32]{1,0:T(1,128)} custom-call(bf16[1,64,8192]{2,1,0:T(8,128)(2,1)} %ta_hbm.1, bf16[1,256,7168]{2,1,0:T(8,128)(2,1)} %tg_hbm.1, bf16[1,4,8192]{2,1,0:T(4,128)(2,1)} %va_hbm.1, bf16[1,4,7168]{2,1,0:T(4,128)(2,1)} %vg_hbm.1), custom_call_target="tpu_custom_call" | custom-call | tf_op jit(solution)/shard_map/pallas_call | solution.py:184
  18.5 1.2 %copy.6 = f32[32]{0:T(128)} copy(f32[32]{0:T(128)} %bitcast.1) | data formatting | bytes 256

commit v3 on v2

--- a/solution.py
+++ b/solution.py
@@ -59,8 +59,6 @@
     load_vg = pltpu.make_async_copy(vg_hbm.at[0], vg.at[d], vg_sem)
     load_ta = pltpu.make_async_copy(ta_hbm.at[0], ta, ta_sem)
     load_tg = pltpu.make_async_copy(tg_hbm.at[0], tg, tg_sem)
-    for load in (load_vg, load_va, load_tg, load_ta):
-        load.start()
 
     barrier = pltpu.get_barrier_semaphore()
     greeted = chain(lambda there: pl.semaphore_signal(barrier, inc=1, device_id=there))
@@ -68,6 +66,8 @@
         pl.semaphore_signal(barrier, inc=1, device_id={"dp": dp_peer(r)[0]})
     for r in range(1, section):
         pl.semaphore_signal(barrier, inc=1, device_id={"section": lax.rem(c + r, section)})
+    for load in (load_vg, load_va, load_tg, load_ta):
+        load.start()
     pl.semaphore_wait(barrier, greeted + len(near) + section - 1)
 
     def val_copy(buf, send, recv, r, k, width, incoming=False):

time: 19.8 us -> 18.4 us (0.929)
  Pallas kernels: 18.4 us -> 17.1 us
    pallas_call x1, Pallas kernels: 18.4 us -> 17.1 us  [local(): pl.pallas_call(functools.partial(kernel, (dp, tensor, section, ca, cg), f...]
where the time goes in v3:
time: 18.4 us; the launch traced here: 18.3 us
  Pallas kernels  17.1 us (93%)
  local copies, waits for them, and re-layouts  1.19 us (6%)
    pallas_call x1, Pallas kernels, local(): pl.pallas_call(functools.partial(kernel, (dp, tensor, section, ca, cg), f...  17.1 us
    unnamed x1, local copies, waits for them, and re-layouts  1.19 us

profile of v3, /device:TPU:0, one launch (start us, length us, event | category | flops | bytes accessed | tf_op | source)
XLA Modules:
  0.0 18.3 jit_solution(7005226249384896347)
XLA Ops:
  0.0 17.1 %shard_map.46 = f32[1,32]{1,0:T(1,128)} custom-call(bf16[1,64,8192]{2,1,0:T(8,128)(2,1)} %ta_hbm.1, bf16[1,256,7168]{2,1,0:T(8,128)(2,1)} %tg_hbm.1, bf16[1,4,8192]{2,1,0:T(4,128)(2,1)} %va_hbm.1, bf16[1,4,7168]{2,1,0:T(4,128)(2,1)} %vg_hbm.1), custom_call_target="tpu_custom_call" | custom-call | tf_op jit(solution)/shard_map/pallas_call | solution.py:184
  17.1 1.2 %copy.6 = f32[32]{0:T(128)} copy(f32[32]{0:T(128)} %bitcast.1) | data formatting | bytes 256

commit v4 on v3

--- a/solution.py
+++ b/solution.py
@@ -61,9 +61,9 @@
     load_tg = pltpu.make_async_copy(tg_hbm.at[0], tg, tg_sem)
 
     barrier = pltpu.get_barrier_semaphore()
-    greeted = chain(lambda there: pl.semaphore_signal(barrier, inc=1, device_id=there))
     for r in near:
         pl.semaphore_signal(barrier, inc=1, device_id={"dp": dp_peer(r)[0]})
+    greeted = chain(lambda there: pl.semaphore_signal(barrier, inc=1, device_id=there))
     for r in range(1, section):
         pl.semaphore_signal(barrier, inc=1, device_id={"section": lax.rem(c + r, section)})
     for load in (load_vg, load_va, load_tg, load_ta):
@@ -93,7 +93,7 @@
             val_copy(vg, vg_send, vg_recv, r, k, wg).start()
     load_va.wait()
     for k in range(ca):
-        for r in near + far:
+        for r in near:
             val_copy(va, va_send, va_recv, r, k, wa).start()
     for s in range(tensor - 2):
         pl.semaphore_wait(z_relay.at[s], greeted)
@@ -106,7 +106,8 @@
         total = None
         for k in range(count):
             for r in near + far:
-                val_copy(buf, send, recv, r, k, width, incoming=True).wait_recv()
+                if not (square and buf is va and r == near[k % 2]):
+                    val_copy(buf, send, recv, r, k, width, incoming=True).wait_recv()
             cols = pl.ds(k * width, width)
             left = jnp.concatenate([buf[j, :, cols] for j in range(dp)], axis=0)
             term = gram_of(left, train[:, cols])
@@ -128,6 +129,20 @@
 
     for r in range(1, tensor):
         grad_copy(r).start()
+
+    def passed_on(k):
+        via = near[k % 2]
+        piece = va.at[dp_peer(via)[1], :, pl.ds(k * wa, wa)]
+        return pltpu.make_async_remote_copy(
+            src_ref=piece, dst_ref=piece,
+            send_sem=va_send.at[2, k], recv_sem=va_recv.at[2, k],
+            device_id={"dp": dp_peer(3 - via)[0]},
+        )
+
+    if square:
+        for k in range(ca):
+            val_copy(va, va_send, va_recv, near[k % 2], k, wa, incoming=True).wait_recv()
+            passed_on(k).start()
 
     load_ta.wait()
     act = gram(va, va_send, va_recv, ta, ca, wa)
@@ -176,7 +191,7 @@
         tokens, hidden = train_grad.shape[1:]
         val = val_act.shape[1]
         factor = 1.0 / math.sqrt(width * hidden * tensor * val * dp)
-        ca, cg = pieces(width, 1), pieces(hidden, 2)
+        ca, cg = pieces(width, 2), pieces(hidden, 2)
         share = tokens // (tensor * section)
         own_lanes = -(-own // LANES) * LANES
         dma = pltpu.SemaphoreType.DMA

time: 18.4 us -> 18.4 us (level)
  no operation moved by 1% of the time
where the time goes in v4:
time: 18.4 us; the launch traced here: 18.2 us
  Pallas kernels  17 us (92%)
  local copies, waits for them, and re-layouts  1.19 us (6%)
    pallas_call x1, Pallas kernels, local(): pl.pallas_call(functools.partial(kernel, (dp, tensor, section, ca, cg), f...  17 us
    unnamed x1, local copies, waits for them, and re-layouts  1.19 us

profile of v4, /device:TPU:0, one launch (start us, length us, event | category | flops | bytes accessed | tf_op | source)
XLA Modules:
  0.0 18.2 jit_solution(9161062858594442216)
XLA Ops:
  0.0 17.0 %shard_map.46 = f32[1,32]{1,0:T(1,128)} custom-call(bf16[1,64,8192]{2,1,0:T(8,128)(2,1)} %ta_hbm.1, bf16[1,256,7168]{2,1,0:T(8,128)(2,1)} %tg_hbm.1, bf16[1,4,8192]{2,1,0:T(4,128)(2,1)} %va_hbm.1, bf16[1,4,7168]{2,1,0:T(4,128)(2,1)} %vg_hbm.1), custom_call_target="tpu_custom_call" | custom-call | tf_op jit(solution)/shard_map/pallas_call | solution.py:199
  17.0 1.2 %copy.6 = f32[32]{0:T(128)} copy(f32[32]{0:T(128)} %bitcast.1) | data formatting | bytes 256
